TPU v7x, 256 devices: a whole 4x4x8 slice. The times are simulated.
256 devices in a mesh: rows: 32 (over x, y, core), cls: 8 (over z).
Axes of the slice: x: 4, y: 4, z: 8, core: 2. Of those that a mesh axis runs over, the one named last changes fastest.
Arguments:
- features: float32 [8, 12288, 512], P('cls', 'rows'), may hold values from -6 to 6
- inverses: float32 [8, 512, 512], P('cls'), may hold values from -1 to 2
- weights: float32 [8, 512, 11264], P(None, 'rows', 'cls'), may hold values from -6 to 6
- residual: float32 [12288, 11264], P('rows', 'cls'), may hold values from -6 to 6
- order: int32 [3], replicated, may hold values from 0 to 7
- owner: int32 [8], replicated, may hold values from 0 to 7, each once
Outputs:
- weights_out: float32 [8, 512, 11264], P(None, 'rows', 'cls')
- residual_out: float32 [12288, 11264], P('rows', 'cls')
Inputs may be any that keep to these rules, and one draw needn't show every extreme that they name: `owner`: each cls index stores exactly one block.
All inputs are finite; a program needn't handle non-finite values.
Results may differ from a plain program's by a relative error of at most 0.00013.
Values sent between devices are 32-bit elements; how exact they have to be, the bound alone decides.
A program may use at most 128 MiB of HBM per device.

v0:
```python
import jax
import jax.numpy as jnp
from jax import lax
from jax.sharding import PartitionSpec as P

STEPS = 3


def spread(shard, axis, root):
    mine = lax.axis_index(axis) == root
    return lax.psum(jnp.where(mine, shard, jnp.zeros_like(shard)), axis)


def body(features, inverses, weights, residual, order, owner):
    highest = lax.Precision.HIGHEST
    total_rows = residual.shape[0] * lax.axis_size("rows")
    penalty = total_rows / 64.0
    inv_rows = 1.0 / total_rows
    share_rows = weights.shape[1]
    block_width = features.shape[2]
    class_width = residual.shape[1]
    position = lax.axis_index("rows")
    for iteration in range(STEPS):
        chosen = order[iteration]
        holder = owner[chosen]
        columns = spread(features[0], "cls", holder)
        inverse = spread(inverses[0], "cls", holder)
        chosen, columns, inverse = (chosen, columns, inverse)

        def correlate(offset, width_now, columns=columns, residual=residual):
            return lax.dot_general(
                columns,
                residual,
                (((0,), (0,)), ((), ())),
                precision=highest,
                preferred_element_type=jnp.float32,
            )

        correlation = lax.psum_scatter(
            correlate(jnp.int32(0), lax.axis_size("rows") * share_rows),
            "rows",
            scatter_dimension=0,
            tiled=True,
        )
        current = lax.dynamic_index_in_dim(weights, chosen, 0, keepdims=False)
        target = correlation - penalty * current

        def absorb(running, piece, offset, inverse=inverse):
            return jnp.dot(inverse, piece, precision=highest, preferred_element_type=jnp.float32)

        empty = jnp.zeros((block_width, class_width), jnp.float32)
        change = (
            absorb(empty, lax.all_gather(target, "rows", axis=0, tiled=True), jnp.int32(0))
            * inv_rows
        )
        own_change = lax.dynamic_slice_in_dim(change, position * share_rows, share_rows, 0)
        residual = residual - jnp.dot(
            columns, change, precision=highest, preferred_element_type=jnp.float32
        )
        weights = lax.dynamic_update_index_in_dim(weights, current + own_change, chosen, 0)
    return (weights, residual)


def solution(mesh):
    return jax.shard_map(
        body,
        mesh=mesh,
        in_specs=(
            P("cls", "rows", None),
            P("cls", None, None),
            P(None, "rows", "cls"),
            P("rows", "cls"),
            P(),
            P(),
        ),
        out_specs=(P(None, "rows", "cls"), P("rows", "cls")),
        check_vma=False,
    )
```

profile of v0, /device:TPU:1, one launch (start us, length us, event | category | flops | bytes accessed | tf_op | source)
XLA Modules:
  0.0 647.9 jit_solution(5150634228960072827)
XLA Ops:
  7.2 0.0 copy-start.11
  7.2 0.0 all-reduce.3.cloned.1.call-start
  7.2 1.2 copy.18
  8.4 1.4 fusion.4
  15.6 1.4 fusion.3
  18.9 2.7 select_bitcast_fusion.3
  21.6 0.0 copy-done.11
  21.6 1.8 select_bitcast_fusion
  23.4 0.0 all-reduce.3.cloned.1.call-update
  23.4 0.0 reduce-scatter.4.cloned.1.call-start
  23.4 139.4 %all-reduce.3.cloned.1.call-done = (f32[512,512]{1,0:T(8,128)}, f32[384,512]{1,0:T(8,128)}, f32[512,512]{1,0:T(8,128)}, f32[384,512]{1,0:T(8,128)}, f32[512,512]{1,0:T(8,128)}, /*index=5*/f32[384,512]{1,0:T(8,128)}) async-done(((f32[512,512]{1,0:T(8,128)}, f32[384,512]{1,0:T(8,128)}, f32[512,512]{1,0:T(8,128)}, f32[384,512]{1,0:T(8,128)}, f32[512,512]{1,0:T(8,128)}, /*index=5*/f32[384,512]{1,0:T(8,128)}), ...) | async-done | bytes 5505040 | tf_op jit(solution)/shard_map/psum | solution.py:11
  162.8 0.0 copy-done.4
  162.8 7.7 %fusion.5 = f32[512,1408]{1,0:T(8,128)} fusion(f32[384,512]{1,0:T(8,128)} %get-tuple-element.3, f32[384,1408]{1,0:T(8,128)S(1)} %copy-done.4), kind=kOutput, calls=%fused_computation.29 | convolution fusion | flops 3321888768 | bytes 5832704 | tf_op jit(solution)/shard_map/dot_general | solution.py:31
  170.5 0.0 reduce-scatter.4.cloned.1.call-update
  170.5 0.0 all-gather.4.cloned.1.call-start
  170.6 84.9 %reduce-scatter.4.cloned.1.call-done = f32[16,1408]{1,0:T(8,128)} async-done(((f32[512,1408]{1,0:T(8,128)}), f32[16,1408]{1,0:T(8,128)}) %reduce-scatter.4.cloned.1.call-update) | async-done | bytes 90128 | tf_op jit(solution)/shard_map/reduce_scatter | solution.py:39
  255.5 1.5 fusion.2
  257.0 0.0 all-gather.4.cloned.1.call-update
  257.1 0.5 reduce-scatter.6.cloned.1.call-start
  257.6 52.8 %all-gather.4.cloned.1.call-done = f32[512,1408]{1,0:T(8,128)} async-done(((f32[16,1408]{1,0:T(8,128)}), f32[512,1408]{1,0:T(8,128)}) %all-gather.4.cloned.1.call-update) | async-done | bytes 2883600 | tf_op jit(solution)/shard_map/all_gather | solution.py:53
  310.3 0.0 copy-done.13
  310.3 7.3 %convolution_multiply_fusion.2 = f32[512,1408]{1,0:T(8,128)S(1)} fusion(f32[512,512]{1,0:T(8,128)S(1)} %copy-done.13, f32[512,1408]{1,0:T(8,128)} %all-gather.4.cloned.1.call-done), kind=kOutput, calls=%fused_computation.2 | convolution fusion | flops 4429905920 | bytes 6815744 | tf_op jit(solution)/shard_map/dot_general | solution.py:49
  317.7 0.0 copy-done.5
  317.7 0.0 copy-done.9
  317.7 0.0 copy-start.2
  317.7 0.0 copy-start.7
  317.7 4.0 convolution_subtract_fusion.2
  321.7 0.0 copy-done.2
  321.7 0.0 copy-done.7
  321.7 6.9 %fusion.6 = f32[512,1408]{1,0:T(8,128)} fusion(f32[384,512]{1,0:T(8,128)S(1)} %copy-done.7, f32[384,1408]{1,0:T(8,128)S(1)} %convolution_subtract_fusion.2), kind=kOutput, calls=%fused_computation.30 | convolution fusion | flops 3321888768 | bytes 5832704 | tf_op jit(solution)/shard_map/dot_general | solution.py:31
  328.6 0.0 reduce-scatter.6.cloned.1.call-update
  328.7 0.0 all-gather.6.cloned.1.call-start
  328.7 0.9 bitcast_dynamic-update-slice_fusion.2
  329.6 0.0 copy-start.10
  329.7 84.2 %reduce-scatter.6.cloned.1.call-done = f32[16,1408]{1,0:T(8,128)} async-done(((f32[512,1408]{1,0:T(8,128)}), f32[16,1408]{1,0:T(8,128)}) %reduce-scatter.6.cloned.1.call-update) | async-done | bytes 90128 | tf_op jit(solution)/shard_map/reduce_scatter | solution.py:39
  413.9 1.5 fusion.1
  415.4 0.0 all-gather.6.cloned.1.call-update
  415.4 0.0 reduce-scatter.8.cloned.1.call-start
  415.5 52.7 %all-gather.6.cloned.1.call-done = f32[512,1408]{1,0:T(8,128)} async-done(((f32[16,1408]{1,0:T(8,128)}), f32[512,1408]{1,0:T(8,128)}) %all-gather.6.cloned.1.call-update) | async-done | bytes 2883600 | tf_op jit(solution)/shard_map/all_gather | solution.py:53
  468.2 0.0 copy-done.10
  468.2 7.5 %convolution_multiply_fusion.1 = f32[512,1408]{1,0:T(8,128)S(1)} fusion(f32[512,512]{1,0:T(8,128)} %get-tuple-element.4, f32[512,1408]{1,0:T(8,128)} %all-gather.6.cloned.1.call-done), kind=kOutput, calls=%fused_computation.1 | convolution fusion | flops 4429905920 | bytes 6815744 | tf_op jit(solution)/shard_map/dot_general | solution.py:49
  475.8 0.0 copy-done.8
  475.8 0.0 copy-start.3
  475.8 0.0 copy-start.6
  475.8 4.0 convolution_subtract_fusion.1
  479.8 0.0 copy-done.3
  479.9 0.0 copy-start
  479.9 1.3 copy-done
  481.2 0.0 copy-done.6
  481.2 6.7 %fusion.7 = f32[512,1408]{1,0:T(8,128)} fusion(f32[384,512]{1,0:T(8,128)S(1)} %copy-done.6, f32[384,1408]{1,0:T(8,128)S(1)} %convolution_subtract_fusion.1), kind=kOutput, calls=%fused_computation.31 | convolution fusion | flops 3321888768 | bytes 5832704 | tf_op jit(solution)/shard_map/dot_general | solution.py:31
  487.9 0.0 reduce-scatter.8.cloned.1.call-update
  488.0 0.0 all-gather.8.cloned.1.call-start
  488.0 1.0 constant_dynamic-slice_fusion
  489.0 1.5 bitcast_dynamic-update-slice_fusion.1
  490.5 82.6 %reduce-scatter.8.cloned.1.call-done = f32[16,1408]{1,0:T(8,128)} async-done(((f32[512,1408]{1,0:T(8,128)}), f32[16,1408]{1,0:T(8,128)}) %reduce-scatter.8.cloned.1.call-update) | async-done | bytes 90128 | tf_op jit(solution)/shard_map/reduce_scatter | solution.py:39
  573.2 1.6 fusion
  574.8 0.0 all-gather.8.cloned.1.call-update
  574.8 0.9 constant_dynamic-slice_fusion.1
  575.7 51.8 %all-gather.8.cloned.1.call-done = f32[512,1408]{1,0:T(8,128)} async-done(((f32[16,1408]{1,0:T(8,128)}), f32[512,1408]{1,0:T(8,128)}) %all-gather.8.cloned.1.call-update) | async-done | bytes 2883600 | tf_op jit(solution)/shard_map/all_gather | solution.py:53
  627.5 0.0 copy-done.12
  627.5 7.3 %convolution_multiply_fusion = f32[512,1408]{1,0:T(8,128)S(1)} fusion(f32[512,512]{1,0:T(8,128)S(1)} %copy-done.12, f32[512,1408]{1,0:T(8,128)} %all-gather.8.cloned.1.call-done), kind=kOutput, calls=%fused_computation | convolution fusion | flops 4429905920 | bytes 6815744 | tf_op jit(solution)/shard_map/dot_general | solution.py:49
  634.8 0.0 copy-done.1
  634.8 5.4 convolution_subtract_fusion
  640.2 0.6 bitcast_dynamic-update-slice_fusion
  (8 shorter events, 0.0 us)
Async XLA Ops:
  7.2 14.4 %copy-start.11 = (f32[1,512,512]{2,1,0:T(8,128)S(1)}, f32[1,512,512]{2,1,0:T(8,128)}, u32[]{:S(2)}) copy-start(f32[1,512,512]{2,1,0:T(8,128)} %param.7) | copy-start | bytes 3145732
  7.2 155.6 %all-reduce.3.cloned.1.call-start = ((), (), s32[]{:S(2)}) async-start(), calls=%async_computation.9 | async-start | bytes 11010048 | tf_op jit(solution)/shard_map/psum | solution.py:11
  23.4 139.4 %copy-start.4 = (f32[384,1408]{1,0:T(8,128)S(1)}, f32[384,1408]{1,0:T(8,128)}, u32[]{:S(2)}) copy-start(f32[384,1408]{1,0:T(8,128)} %param.9) | copy-start | bytes 6488068
  23.4 232.1 %reduce-scatter.4.cloned.1.call-start = ((), (), s32[]{:S(2)}) async-start(), calls=%async_computation.3 | async-start | bytes 2973696 | tf_op jit(solution)/shard_map/reduce_scatter | solution.py:39
  170.5 139.8 %copy-start.13 = (f32[512,512]{1,0:T(8,128)S(1)}, f32[512,512]{1,0:T(8,128)}, u32[]{:S(2)}) copy-start(f32[512,512]{1,0:T(8,128)} %get-tuple-element.2) | copy-start | bytes 3145732
  170.5 139.8 %all-gather.4.cloned.1.call-start = ((), (), s32[]{:S(2)}) async-start(), calls=%async_computation.4 | async-start | bytes 2973696 | tf_op jit(solution)/shard_map/all_gather | solution.py:53
  257.1 156.8 %reduce-scatter.6.cloned.1.call-start = ((), (), s32[]{:S(2)}) async-start(), calls=%async_computation.5 | async-start | bytes 2973696 | tf_op jit(solution)/shard_map/reduce_scatter | solution.py:39
  310.3 7.3 %copy-start.5 = (f32[384,1408]{1,0:T(8,128)S(1)}, f32[384,1408]{1,0:T(8,128)}, u32[]{:S(2)}) copy-start(f32[384,1408]{1,0:T(8,128)} %param.9) | copy-start | bytes 6488068
  310.3 7.3 %copy-start.9 = (f32[384,512]{1,0:T(8,128)S(1)}, f32[384,512]{1,0:T(8,128)}, u32[]{:S(2)}) copy-start(f32[384,512]{1,0:T(8,128)} %get-tuple-element.3) | copy-start | bytes 2359300
  317.7 4.0 copy-start.2
  317.7 4.0 copy-start.7
  328.7 139.6 %all-gather.6.cloned.1.call-start = ((), (), s32[]{:S(2)}) async-start(), calls=%async_computation.6 | async-start | bytes 2973696 | tf_op jit(solution)/shard_map/all_gather | solution.py:53
  329.6 138.6 %copy-start.10 = (f32[8,16,1408]{2,1,0:T(8,128)}, f32[8,16,1408]{2,1,0:T(8,128)S(1)}, u32[]{:S(2)}) copy-start(f32[8,16,1408]{2,1,0:T(8,128)S(1)} %bitcast_dynamic-update-slice_fusion.2) | copy-start | bytes 2162692
  415.4 157.7 %reduce-scatter.8.cloned.1.call-start = ((), (), s32[]{:S(2)}) async-start(), calls=%async_computation.7 | async-start | bytes 2973696 | tf_op jit(solution)/shard_map/reduce_scatter | solution.py:39
  468.2 7.6 %copy-start.8 = (f32[384,512]{1,0:T(8,128)S(1)}, f32[384,512]{1,0:T(8,128)}, u32[]{:S(2)}) copy-start(f32[384,512]{1,0:T(8,128)} %get-tuple-element.5) | copy-start | bytes 2359300
  475.8 4.1 copy-start.3
  475.8 5.4 copy-start.6
  479.9 1.3 copy-start
  487.9 139.5 %copy-start.12 = (f32[512,512]{1,0:T(8,128)S(1)}, f32[512,512]{1,0:T(8,128)}, u32[]{:S(2)}) copy-start(f32[512,512]{1,0:T(8,128)} %get-tuple-element.6) | copy-start | bytes 3145732
  488.0 139.5 %all-gather.8.cloned.1.call-start = ((), (), s32[]{:S(2)}) async-start(), calls=%async_computation.8 | async-start | bytes 2973696 | tf_op jit(solution)/shard_map/all_gather | solution.py:53
  627.5 7.3 %copy-start.1 = (f32[384,1408]{1,0:T(8,128)S(1)}, f32[384,1408]{1,0:T(8,128)}, u32[]{:S(2)}) copy-start(f32[384,1408]{1,0:T(8,128)} %copy-done) | copy-start | bytes 6488068
Sparse Core Ops, SparseCore 0:
  23.5 139.2 all-reduce.2
  170.6 84.8 reduce-scatter.3
  258.9 51.3 all-gather.3
  328.8 85.0 reduce-scatter.5
  416.8 51.3 all-gather.5
  488.1 85.0 reduce-scatter.7
  576.0 51.3 all-gather.7
where the time goes:
time: 653 us; the launch traced here: 648 us
  waiting for transfers between devices  549 us (84%)
  matrix products  56.9 us (9%)
  between operations  22.3 us (3%)
  other arithmetic  12.2 us (2%)
  local copies, waits for them, and re-layouts  7.23 us (1%)
    reduce_scatter x3, waiting for transfers between devices, body(): lax.psum_scatter(correlate(jnp.int32(0), lax.axis_size('rows') * share_ro...  252 us
    all_gather x3, waiting for transfers between devices, body(): lax.all_gather(target, 'rows', axis=0, tiled=True)  157 us
    psum x1, waiting for transfers between devices, spread(): return lax.psum(jnp.where(mine, shard, jnp.zeros_like(shard)), axis)  139 us
    dot_general x3, matrix products, absorb(): jnp.dot(inverse, piece, precision=highest, preferred_element_type=jnp.flo...  22.1 us
    dot_general x3, matrix products, correlate(): lax.dot_general(columns, residual, (((0,), (0,)), ((), ())), precision=hi...  21.3 us
    dot_general x3, matrix products, body(): jnp.dot(columns, change, precision=highest, preferred_element_type=jnp.fl...  13.4 us
  transfers between devices with their start and end apart: 7, of which 7 were waited for; matrix products, arithmetic and copies ran while one was open for 1% of the time, Pallas kernels for 0%

commit v1 on v0

v1 whole, which is shorter than its diff:
```python
import functools

import jax
import jax.numpy as jnp
from jax import lax
from jax.experimental import pallas as pl
from jax.experimental.pallas import tpu as pltpu
from jax.sharding import PartitionSpec as P

STEPS = 3
MESH = pl.DeviceIdType.MESH
F32 = jnp.float32
BF16 = jnp.bfloat16


def split(value):
    high = value.astype(BF16)
    return high, (value - high.astype(F32)).astype(BF16)


def plan(chip_rows):
    eighths = chip_rows // 8
    first = (eighths + 1) // 2
    return (8 * first, 8 * (eighths - first))


def kernel(side, depth, parts, chosen_ref, holder_ref, x_ref, f_ref, i_ref, out_ref, *scratch):
    count = len(parts)
    (pz, stage, fbuf, iz, invf, wide, wide_low, wide_back, inv_high, inv_low) = scratch[:10]
    (z_send, z_recv, i_send, i_recv, c_send, c_recv, t_send, t_recv) = scratch[10:18]
    per_part = scratch[18:]
    cbuf, cother, rs1x, rs1y, t1x, t1y, rs2x, rs2y, tfull, dfull = (
        per_part[k * count : (k + 1) * count] for k in range(10)
    )
    rows = f_ref.shape[0]
    half = f_ref.shape[1] // 2
    quarter = half // 2
    total_rows = rows * side * side * 2
    penalty = total_rows / 64.0
    inv_rows = 1.0 / total_rows
    share = i_ref.shape[0]
    piece = rows // depth

    r = lax.axis_index("rows")
    mz = lax.axis_index("cls")
    core = lax.rem(r, 2)
    other = 1 - core
    my = lax.rem(lax.div(r, 2), side)
    mx = lax.div(r, 2 * side)

    def at_x(d):
        return ((lax.rem(mx + d, side) * side + my) * 2 + core, mz)

    def at_y(d):
        return ((mx * side + lax.rem(my + d, side)) * 2 + core, mz)

    def at_z(d):
        return (r, lax.rem(mz + d, depth))

    partner = ((mx * side + my) * 2 + other, mz)

    barrier = pltpu.get_barrier_semaphore()
    peers = (
        [at_x(d) for d in range(1, side)]
        + [at_y(d) for d in range(1, side)]
        + [at_z(d) for d in range(1, depth)]
        + [partner]
    )
    for peer in peers:
        pl.semaphore_signal(barrier, inc=1, device_id=peer, device_id_type=MESH)
    pl.semaphore_wait(barrier, len(peers))

    def remote(src, dst, send, recv, device):
        copy = pltpu.make_async_remote_copy(
            src_ref=src, dst_ref=dst, send_sem=send, recv_sem=recv, device_id=device, device_id_type=MESH
        )
        copy.start()
        return copy

    def finish(copies):
        for copy in copies:
            copy.wait()

    first_copies, inverse_copies = [], []
    for d in range(1, depth):
        to = lax.rem(mz + d, depth)
        first_copies.append(
            remote(f_ref.at[pl.ds(to * piece, piece)], pz.at[mz], z_send.at[0, d - 1], z_recv.at[0, d - 1], at_z(d))
        )
    for d in range(1, depth):
        inverse_copies.append(remote(i_ref, iz.at[mz], z_send.at[1, d - 1], z_recv.at[1, d - 1], at_z(d)))
    pz[mz] = f_ref[pl.ds(mz * piece, piece)]
    iz[mz] = i_ref[...]
    out_ref[...] = x_ref[...]
    finish(first_copies)

    def send_block(s):
        value = pz[holder_ref[s]]
        stage[s] = value
        fbuf[s, mz] = value
        return [
            remote(stage.at[s], fbuf.at[s, mz], z_send.at[2 + s, d - 1], z_recv.at[2 + s, d - 1], at_z(d))
            for d in range(1, depth)
        ]

    block_copies = {0: send_block(0)}

    finish(inverse_copies)
    for s in range(STEPS):
        invf[s, mx, my] = iz[holder_ref[s]]
    low, high = pl.ds(0, half), pl.ds(half, half)
    copies = []
    for d in range(1, side):
        src = invf.at[:, mx, my, :, low]
        copies.append(remote(src, src, i_send.at[0, d - 1], i_recv.at[0, d - 1], at_x(d)))
        src = invf.at[:, mx, my, :, high]
        copies.append(remote(src, src, i_send.at[1, d - 1], i_recv.at[1, d - 1], at_y(d)))
    finish(copies)
    copies = []
    for d in range(1, side):
        src = invf.at[:, :, my, :, low]
        copies.append(remote(src, src, i_send.at[2, d - 1], i_recv.at[2, d - 1], at_y(d)))
        src = invf.at[:, mx, :, :, high]
        copies.append(remote(src, src, i_send.at[3, d - 1], i_recv.at[3, d - 1], at_x(d)))
    finish(copies)

    def dot(a, b):
        return jnp.dot(a, b, preferred_element_type=F32)

    def dot_back(a, b):
        return lax.dot_general(a, b, (((1,), (1,)), ((), ())), preferred_element_type=F32)

    def three(product, a, b_high, b_low):
        a_high, a_low = a
        return product(a_high, b_high) + (product(a_high, b_low) + product(a_low, b_high))

    def prepare(s):
        finish(block_copies[s])
        slot = s % 2
        extra = out_ref.shape[1] - rows
        place = lax.broadcasted_iota(jnp.int32, (extra, half), 0) - share * chosen_ref[s]
        inside = (place >= 0) & (place < share)
        lane = lax.broadcasted_iota(jnp.int32, (extra, half), 1)
        for h in range(2):
            f_high, f_low = split(fbuf[s, :, :, h * half : (h + 1) * half].reshape(rows, half))
            hit = inside & (share * r + place == lane + h * half)
            wide[slot, h, :rows] = f_high
            wide_back[slot, h, :rows] = f_high
            wide_low[slot, h, :rows] = f_low
            wide[slot, h, rows:] = jnp.where(hit, -penalty, 0.0).astype(BF16)
            wide_back[slot, h, rows:] = jnp.where(hit, -1.0, 0.0).astype(BF16)
            wide_low[slot, h, rows:] = jnp.zeros((extra, half), BF16)
        i_high, i_low = split(invf[s].reshape(half, 2 * half))
        inv_high[slot] = i_high
        inv_low[slot] = i_low

    offsets = [side * side * sum(parts[:c]) for c in range(count)]
    live = {}

    def correlate(s, c):
        slot, size = s % 2, side * side * parts[c]
        x = split(out_ref[offsets[c] : offsets[c] + size, :])
        shape = (side, side, parts[c], half)
        cbuf[c][other] = three(dot, x, wide[slot, other], wide_low[slot, other]).reshape(shape)
        live[c] = [remote(cbuf[c].at[other], cother[c], c_send.at[0, c], c_recv.at[0, c], partner)]
        cbuf[c][core] = three(dot, x, wide[slot, core], wide_low[slot, core]).reshape(shape)

    def scatter_first(s, c):
        finish(live[c])
        cbuf[c][core] = cbuf[c][core] + cother[c][...]
        live[c] = []
        for d in range(1, side):
            src = cbuf[c].at[core, lax.rem(mx + d, side), :, :, pl.ds(0, quarter)]
            live[c].append(remote(src, rs1x[c].at[d - 1], t_send.at[0, c, d - 1], t_recv.at[0, c, d - 1], at_x(d)))
            src = cbuf[c].at[core, :, lax.rem(my + d, side), :, pl.ds(quarter, quarter)]
            live[c].append(remote(src, rs1y[c].at[d - 1], t_send.at[1, c, d - 1], t_recv.at[1, c, d - 1], at_y(d)))

    def scatter_second(s, c):
        finish(live[c])
        live[c] = []
        sum_x = cbuf[c][core, mx, :, :, :quarter]
        sum_y = cbuf[c][core, :, my, :, quarter:]
        for d in range(1, side):
            sum_x = sum_x + rs1x[c][d - 1]
            sum_y = sum_y + rs1y[c][d - 1]
        t1x[c][...] = sum_x
        t1y[c][...] = sum_y
        for d in range(1, side):
            src = t1x[c].at[lax.rem(my + d, side)]
            live[c].append(remote(src, rs2x[c].at[d - 1], t_send.at[2, c, d - 1], t_recv.at[2, c, d - 1], at_y(d)))
            src = t1y[c].at[lax.rem(mx + d, side)]
            live[c].append(remote(src, rs2y[c].at[d - 1], t_send.at[3, c, d - 1], t_recv.at[3, c, d - 1], at_x(d)))

    def target(s, c):
        finish(live[c])
        sum_x = t1x[c][my]
        sum_y = t1y[c][mx]
        for d in range(1, side):
            sum_x = sum_x + rs2x[c][d - 1]
            sum_y = sum_y + rs2y[c][d - 1]
        tfull[c][core, :, :quarter] = sum_x
        tfull[c][core, :, quarter:] = sum_y
        live[c] = [remote(tfull[c].at[core], tfull[c].at[core], c_send.at[1, c], c_recv.at[1, c], partner)]

    def solve(s, c):
        finish(live[c])
        slot = s % 2
        change = three(dot_back, split(tfull[c][0]), inv_high[slot, :, :half], inv_low[slot, :, :half])
        change += three(dot_back, split(tfull[c][1]), inv_high[slot, :, half:], inv_low[slot, :, half:])
        dfull[c][core, mx, my] = change * inv_rows
        live[c] = []
        for d in range(1, side):
            src = dfull[c].at[core, mx, my, :, pl.ds(0, quarter)]
            live[c].append(remote(src, src, t_send.at[4, c, d - 1], t_recv.at[4, c, d - 1], at_x(d)))
            src = dfull[c].at[core, mx, my, :, pl.ds(quarter, quarter)]
            live[c].append(remote(src, src, t_send.at[5, c, d - 1], t_recv.at[5, c, d - 1], at_y(d)))

    def gather_second(s, c):
        finish(live[c])
        live[c] = []
        for d in range(1, side):
            src = dfull[c].at[core, :, my, :, pl.ds(0, quarter)]
            live[c].append(remote(src, src, t_send.at[6, c, d - 1], t_recv.at[6, c, d - 1], at_y(d)))
            src = dfull[c].at[core, mx, :, :, pl.ds(quarter, quarter)]
            live[c].append(remote(src, src, t_send.at[7, c, d - 1], t_recv.at[7, c, d - 1], at_x(d)))

    def swap(s, c):
        finish(live[c])
        live[c] = [remote(dfull[c].at[core], dfull[c].at[core], c_send.at[2, c], c_recv.at[2, c], partner)]

    def update(s, c):
        finish(live[c])
        slot, size = s % 2, side * side * parts[c]
        gone = 0.0
        for h in range(2):
            d = split(dfull[c][h].reshape(size, half))
            gone = gone + three(dot_back, d, wide_back[slot, h], wide_low[slot, h])
        at = slice(offsets[c], offsets[c] + size)
        out_ref[at, :] = out_ref[at, :] - gone

    phases = [correlate, scatter_first, scatter_second, target, solve, gather_second, swap, update]
    lag = max(1, len(phases) // count)
    for tick in range(STEPS * len(phases) + lag * (count - 1)):
        for c in range(count):
            at = tick - lag * c
            if not 0 <= at < STEPS * len(phases):
                continue
            s, phase = divmod(at, len(phases))
            if c == 0 and phase == 0:
                prepare(s)
                if s + 1 < STEPS:
                    block_copies[s + 1] = send_block(s + 1)
            phases[phase](s, c)


def body(side, depth, features, inverses, weights, residual, order, owner):
    rows, classes = residual.shape
    width = features.shape[2]
    half, quarter = width // 2, width // 4
    share = weights.shape[1]
    chips = side * side
    parts = plan(classes // chips)
    r = lax.axis_index("rows")
    begin = lax.rem(r, 2) * half + lax.div(r, 2) * share
    inverse = lax.dynamic_slice_in_dim(inverses[0], begin, share, 0)
    stored = weights.reshape(weights.shape[0] * share, classes)
    state = jnp.concatenate([residual, stored], axis=0).T
    deep = state.shape[1]
    piece = rows // depth
    scratch = [
        pltpu.VMEM((depth, piece, width), F32),
        pltpu.VMEM((STEPS, piece, width), F32),
        pltpu.VMEM((STEPS, depth, piece, width), F32),
        pltpu.VMEM((depth, share, width), F32),
        pltpu.VMEM((STEPS, side, side, share, width), F32),
        pltpu.VMEM((2, 2, deep, half), BF16),
        pltpu.VMEM((2, 2, deep, half), BF16),
        pltpu.VMEM((2, 2, deep, half), BF16),
        pltpu.VMEM((2, half, width), BF16),
        pltpu.VMEM((2, half, width), BF16),
        pltpu.SemaphoreType.DMA((2 + STEPS, depth - 1)),
        pltpu.SemaphoreType.DMA((2 + STEPS, depth - 1)),
        pltpu.SemaphoreType.DMA((4, side - 1)),
        pltpu.SemaphoreType.DMA((4, side - 1)),
        pltpu.SemaphoreType.DMA((3, len(parts))),
        pltpu.SemaphoreType.DMA((3, len(parts))),
        pltpu.SemaphoreType.DMA((8, len(parts), side - 1)),
        pltpu.SemaphoreType.DMA((8, len(parts), side - 1)),
    ]
    for shape in (
        lambda p: (2, side, side, p, half),
        lambda p: (side, side, p, half),
        lambda p: (side - 1, side, p, quarter),
        lambda p: (side - 1, side, p, quarter),
        lambda p: (side, p, quarter),
        lambda p: (side, p, quarter),
        lambda p: (side - 1, p, quarter),
        lambda p: (side - 1, p, quarter),
        lambda p: (2, p, half),
        lambda p: (2, side, side, p, half),
    ):
        scratch += [pltpu.VMEM(shape(p), F32) for p in parts]
    vmem = pl.BlockSpec(memory_space=pltpu.VMEM)
    smem = pl.BlockSpec(memory_space=pltpu.SMEM)
    state = pl.pallas_call(
        functools.partial(kernel, side, depth, parts),
        out_shape=jax.ShapeDtypeStruct(state.shape, F32),
        in_specs=[smem, smem, vmem, vmem, vmem],
        out_specs=vmem,
        scratch_shapes=scratch,
        compiler_params=pltpu.CompilerParams(collective_id=0, has_side_effects=True, vmem_limit_bytes=56 << 20),
        cost_estimate=pl.CostEstimate(flops=14 * 10**9, bytes_accessed=8 * 10**6, transcendentals=0),
    )(order, owner[order], state, features[0], inverse)
    back = state.T
    return back[rows:].reshape(weights.shape), back[:rows]


def solution(mesh):
    side = {32: 4, 8: 2}[mesh.shape["rows"]]
    return jax.shard_map(
        functools.partial(body, side, mesh.shape["cls"]),
        mesh=mesh,
        in_specs=(
            P("cls", "rows", None),
            P("cls", None, None),
            P(None, "rows", "cls"),
            P("rows", "cls"),
            P(),
            P(),
        ),
        out_specs=(P(None, "rows", "cls"), P("rows", "cls")),
        check_vma=False,
    )
```

time: 653 us -> 200 us (0.31)
  waiting for transfers between devices: 549 us -> 0 us
  Pallas kernels: 0 us -> 180 us
  matrix products: 56.9 us -> 0 us
  between operations: 22.3 us -> 0.67 us
  other arithmetic: 12.2 us -> 3.81 us
  local copies, waits for them, and re-layouts: 7.23 us -> 15 us
    reduce_scatter x3 -> x0, waiting for transfers between devices: 252 us -> none  [body(): lax.psum_scatter(correlate(jnp.int32(0), lax.axis_size('rows') * share_ro...]
    pallas_call x0 -> x1, Pallas kernels: none -> 180 us  [body(): pl.pallas_call(functools.partial(kernel, side, depth, parts), out_shape=j...]
    all_gather x3 -> x0, waiting for transfers between devices: 157 us -> none  [body(): lax.all_gather(target, 'rows', axis=0, tiled=True)]
    psum x1 -> x0, waiting for transfers between devices: 139 us -> none  [spread(): return lax.psum(jnp.where(mine, shard, jnp.zeros_like(shard)), axis)]
    dot_general x9 -> x0, matrix products: 56.9 us -> none  [the longest x3 22.1 us: absorb(): jnp.dot(inverse, piece, precision=highest, preferred_element_type=jnp.flo...]
  transfers between devices with their start and end apart: 7 -> 0, of which waited for: 7 -> 0; matrix products, arithmetic and copies ran while one was open for 1% -> 0% of each run, Pallas kernels for 0% -> 0%
where the time goes in v1:
time: 200 us; the launch traced here: 199 us
  Pallas kernels  180 us (90%)
  local copies, waits for them, and re-layouts  15 us (8%)
  other arithmetic  3.81 us (2%)
    pallas_call x1, Pallas kernels, body(): pl.pallas_call(functools.partial(kernel, side, depth, parts), out_shape=j...  180 us
    slice x3, local copies, waits for them, and re-layouts, body(): return (back[rows:].reshape(weights.shape), back[:rows])  6.01 us
    unnamed x4, local copies, waits for them, and re-layouts  4.31 us

profile of v1, /device:TPU:1, one launch (start us, length us, event | category | flops | bytes accessed | tf_op | source)
XLA Modules:
  0.0 199.4 jit_solution(2329609740613019263)
XLA Ops:
  0.6 0.0 copy-start
  0.7 0.7 compare_select_fusion
  1.4 1.8 gather_fusion
  3.2 0.0 copy-done
  3.2 0.6 dynamic-slice_bitcast_fusion.i_ref
  3.8 2.2 %copy.13 = f32[128,1408]{0,1:T(8,128)} copy(f32[128,1408]{1,0:T(8,128)} %bitcast.10) | data formatting | bytes 1441792 | tf_op jit(solution)/shard_map/reshape | solution.py:266
  6.1 2.3 %copy.12 = f32[384,1408]{0,1:T(8,128)S(1)} copy(f32[384,1408]{1,0:T(8,128)} %param.9) | data formatting | bytes 4325376 | tf_op args[3]
  8.4 3.1 %maximum_bitcast_fusion.x_ref = f32[1408,512]{1,0:T(8,128)} fusion(f32[128,1408]{0,1:T(8,128)} %copy.13, f32[384,1408]{0,1:T(8,128)S(1)} %copy.12), kind=kLoop, calls=%fused_computation.1 | loop fusion | flops 720896 | bytes 5767168 | tf_op jit(solution)/shard_map/transpose | solution.py:267
  11.4 179.9 %shard_map.77 = f32[1408,512]{1,0:T(8,128)} custom-call(s32[3]{0:T(128)} %chosen_ref.1, s32[3]{0:T(128)} %gather_fusion, f32[1408,512]{1,0:T(8,128)} %maximum_bitcast_fusion.x_ref, f32[384,512]{1,0:T(8,128)} %bitcast.12, f32[16,512]{1,0:T(8,128)} %dynamic-slice_bitcast_fusion.i_ref), custom_call_target="tpu_custom_call" | custom-call | flops 14000000000 | bytes 8000000 | tf_op jit(solution)/shard_map/pallas_call | solution.py:305
  191.3 2.0 %slice.10 = f32[128,1408]{0,1:T(8,128)} slice(f32[512,1408]{0,1:T(8,128)} %bitcast.8), slice={[384:512], [0:1408]} | slice | bytes 1441792 | tf_op jit(solution)/shard_map/slice | solution.py:315
  193.4 1.7 slice.11
  195.1 2.0 %copy.15 = f32[384,1408]{1,0:T(8,128)} copy(f32[384,1408]{0,1:T(8,128)S(1)} %slice.11) | data formatting | bytes 4325376
  197.1 2.2 %copy.14 = f32[128,1408]{1,0:T(8,128)} copy(f32[128,1408]{0,1:T(8,128)} %slice.10) | data formatting | bytes 1441792 | tf_op jit(solution)/shard_map/slice | solution.py:315
  (1 shorter events, 0.0 us)
Async XLA Ops:
  0.6 2.6 %copy-start = (f32[1,512,512]{2,1,0:T(8,128)S(1)}, f32[1,512,512]{2,1,0:T(8,128)}, u32[]{:S(2)}) copy-start(f32[1,512,512]{2,1,0:T(8,128)} %param.7) | copy-start | bytes 3145732

commit v2 on v1

v2 whole, which is shorter than its diff:
```python
import functools

import jax
import jax.numpy as jnp
from jax import lax
from jax.experimental import pallas as pl
from jax.experimental.pallas import tpu as pltpu
from jax.sharding import PartitionSpec as P

STEPS = 3
MESH = pl.DeviceIdType.MESH
F32 = jnp.float32
BF16 = jnp.bfloat16


def split(value):
    high = value.astype(BF16)
    return high, (value - high.astype(F32)).astype(BF16)


def plan(chip_rows):
    eighths = chip_rows // 8
    count = min(4, eighths)
    return tuple(8 * (eighths // count + (c < eighths % count)) for c in range(count))


PHASES = 8
PREPARE = 8
GATHER = 9


def schedule(parts, depth):
    total = sum(parts)
    works = [c / total for c in parts]
    compute = (4.5, 0.8, 0.5, 0.2, 1.5, 0.0, 0.0, 4.5)
    fixed = (0.1, 0.4, 0.4, 0.2, 0.5, 0.4, 0.1, 0.1)
    moves = ((0, 3.4), (1, 7.2), (1, 1.8), (0, 0.2), (1, 1.8), (1, 7.2), (0, 3.4), None)
    delay = (1.0, 2.5)
    free = [0.0, 0.0]
    now = 0.0
    ready = [0.0] * len(parts)
    place = [0] * len(parts)
    gather_ready, gather_place = 6.0, 0
    block_ready = [0.0] + [18.0 * s for s in range(1, STEPS)]
    prepared, done, solved = 0, [0] * STEPS, [0] * STEPS
    order = []
    while min(place) < STEPS * PHASES:
        options = []
        for c in range(len(parts)):
            if place[c] == STEPS * PHASES:
                continue
            s, phase = divmod(place[c], PHASES)
            if phase == 0 and prepared <= s:
                continue
            if phase == 4 and gather_place < 3 * s + 3:
                continue
            options.append((max(ready[c], now), place[c], phase, s, c))
        if prepared < STEPS and (prepared < 2 or done[prepared - 2] == len(parts)):
            if any(p == prepared * PHASES for p in place):
                options.append((max(block_ready[prepared], now), -1, PREPARE, prepared, 0))
        s, stage = divmod(gather_place, 3)
        if s < STEPS and (stage < 2 or s < 2 or solved[s - 2] == len(parts)) and max(place) >= (s - 1) * PHASES + 2:
            options.append((max(gather_ready, now), s * PHASES + 3, GATHER + stage, s, 0))
        start, _, kind, s, c = min(options)
        order.append((kind, s, c))
        now = start
        if kind == PREPARE:
            now += 1.0
            prepared += 1
        elif kind >= GATHER:
            now += 0.5
            if kind < GATHER + 2:
                free[1] = max(free[1], now) + (0.7, 2.6)[kind - GATHER]
                gather_ready = free[1] + delay[1]
            gather_place += 1
        else:
            now += compute[kind] * works[c] + fixed[kind]
            place[c] += 1
            ready[c] = now
            if moves[kind]:
                link, long = moves[kind]
                free[link] = max(free[link], now) + long * works[c]
                ready[c] = free[link] + delay[link]
            done[s] += kind == PHASES - 1
            solved[s] += kind == 4
    return order


def kernel(side, depth, parts, chosen_ref, owner_ref, f_ref, all_inverse, w_in, r_in, w_out, r_out, *scratch):
    count = len(parts)
    (i_ref, w_ref, r_ref, w_back, r_back, out_ref) = scratch[:6]
    (pz, stage, fbuf, iz, invf, wide, wide_low, wide_back, inv_high, inv_low) = scratch[6:16]
    (z_send, z_recv, i_send, i_recv, c_send, c_recv, t_send, t_recv, l_sem) = scratch[16:25]
    per_part = scratch[25:]
    cbuf, cother, rs1, t1x, t1y, rs2, tfull, dfull = (per_part[k * count : (k + 1) * count] for k in range(8))
    rows, width = f_ref.shape[1:]
    half = width // 2
    quarter = half // 2
    total_rows = rows * side * side * 2
    penalty = total_rows / 64.0
    inv_rows = 1.0 / total_rows
    share = i_ref.shape[0]
    blocks = w_in.shape[0]
    piece = rows // depth

    r = lax.axis_index("rows")
    mz = lax.axis_index("cls")
    core = lax.rem(r, 2)
    other = 1 - core
    my = lax.rem(lax.div(r, 2), side)
    mx = lax.div(r, 2 * side)

    def at_x(d):
        return ((lax.rem(mx + d, side) * side + my) * 2 + core, mz)

    def at_y(d):
        return ((mx * side + lax.rem(my + d, side)) * 2 + core, mz)

    def at_z(d):
        return (r, lax.rem(mz + d, depth))

    partner = ((mx * side + my) * 2 + other, mz)

    begin = pl.multiple_of(core * half + (mx * side + my) * share, share)
    load_inverse = pltpu.make_async_copy(all_inverse.at[0, pl.ds(begin, share)], i_ref, l_sem.at[0])
    load_inverse.start()
    load_r = pltpu.make_async_copy(r_in, r_ref, l_sem.at[1])
    load_r.start()
    load_w = pltpu.make_async_copy(w_in, w_ref, l_sem.at[2])
    load_w.start()

    barrier = pltpu.get_barrier_semaphore()
    peers = (
        [at_x(d) for d in range(1, side)]
        + [at_y(d) for d in range(1, side)]
        + [at_z(d) for d in range(1, depth)]
        + [partner]
    )
    for peer in peers:
        pl.semaphore_signal(barrier, inc=1, device_id=peer, device_id_type=MESH)
    pl.semaphore_wait(barrier, len(peers))

    def remote(src, dst, send, recv, device):
        copy = pltpu.make_async_remote_copy(
            src_ref=src, dst_ref=dst, send_sem=send, recv_sem=recv, device_id=device, device_id_type=MESH
        )
        copy.start()
        return copy

    def joint(ref, send, recv):
        return pltpu.make_async_remote_copy(
            src_ref=ref, dst_ref=ref, send_sem=send, recv_sem=recv, device_id=partner, device_id_type=MESH
        )

    for d in range(1, depth):
        to = lax.rem(mz + d, depth)
        src = f_ref.at[0, pl.ds(to * piece, piece)]
        remote(src, pz.at[mz], z_send.at[0], z_recv.at[0], at_z(d))
    pz[mz] = f_ref[0, pl.ds(mz * piece, piece)]

    def send_block(s):
        value = pz[owner_ref[chosen_ref[s]]]
        stage[s] = value
        fbuf[s, mz] = value
        for d in range(1, depth):
            remote(stage.at[s], fbuf.at[s, mz], z_send.at[2 + s], z_recv.at[2 + s], at_z(d))

    offsets = [side * side * sum(parts[:c]) for c in range(count)]
    def send_inverse():
        load_inverse.wait()
        for d in range(1, depth):
            remote(i_ref, iz.at[mz], z_send.at[1], z_recv.at[1], at_z(d))
        iz[mz] = i_ref[...]

    def turn_over(c):
        size = side * side * parts[c]
        at = slice(offsets[c], offsets[c] + size)
        out_ref[at, :rows] = r_ref[:, at].T
        out_ref[at, rows:] = w_ref[:, :, at].reshape(blocks * share, size).T

    others = pl.ds(0, depth - 1)
    joint(pz.at[others], z_send.at[0], z_recv.at[0]).wait()
    send_block(0)
    send_inverse()
    load_r.wait()
    load_w.wait()
    for c in range(count):
        turn_over(c)

    low, high = pl.ds(0, half), pl.ds(half, half)

    def inverse_first(s):
        if s == 0:
            joint(iz.at[others], z_send.at[1], z_recv.at[1]).wait()
        invf[s, mx, my] = iz[owner_ref[chosen_ref[s]]]
        for d in range(1, side):
            src = invf.at[s, mx, my, :, low]
            remote(src, src, i_send.at[s, 0], i_recv.at[s, 0], at_x(d))
            src = invf.at[s, mx, my, :, high]
            remote(src, src, i_send.at[s, 0], i_recv.at[s, 0], at_y(d))

    def inverse_second(s):
        joint(iz.at[pl.ds(0, side - 1)], i_send.at[s, 0], i_recv.at[s, 0]).wait()
        for d in range(1, side):
            src = invf.at[s, :, my, :, low]
            remote(src, src, i_send.at[s, 1], i_recv.at[s, 1], at_y(d))
            src = invf.at[s, mx, :, :, high]
            remote(src, src, i_send.at[s, 1], i_recv.at[s, 1], at_x(d))

    def inverse_third(s):
        joint(invf.at[s, pl.ds(0, side - 1)], i_send.at[s, 1], i_recv.at[s, 1]).wait()
        slot = s % 2
        i_high, i_low = split(invf[s].reshape(half, 2 * half))
        inv_high[slot] = i_high
        inv_low[slot] = i_low

    def dot(a, b):
        return jnp.dot(a, b, preferred_element_type=F32)

    def dot_back(a, b):
        return lax.dot_general(a, b, (((1,), (1,)), ((), ())), preferred_element_type=F32)

    def three(product, a, b_high, b_low):
        a_high, a_low = a
        return product(a_high, b_high) + (product(a_high, b_low) + product(a_low, b_high))

    def prepare(s):
        joint(fbuf.at[s, others], z_send.at[2 + s], z_recv.at[2 + s]).wait()
        if s + 1 < STEPS:
            send_block(s + 1)
        slot = s % 2
        extra = out_ref.shape[1] - rows
        place = lax.broadcasted_iota(jnp.int32, (extra, half), 0) - share * chosen_ref[s]
        inside = (place >= 0) & (place < share)
        lane = lax.broadcasted_iota(jnp.int32, (extra, half), 1)
        block = fbuf[s].reshape(rows, width)
        for h in range(2):
            f_high, f_low = split(block[:, h * half : (h + 1) * half])
            hit = inside & (share * r + place == lane + h * half)
            wide[slot, h, :rows] = f_high
            wide_back[slot, h, :rows] = f_high
            wide_low[slot, h, :rows] = f_low
            wide[slot, h, rows:] = jnp.where(hit, -penalty, 0.0).astype(BF16)
            wide_back[slot, h, rows:] = jnp.where(hit, -1.0, 0.0).astype(BF16)
            wide_low[slot, h, rows:] = jnp.zeros((extra, half), BF16)

    live = {}
    stores = []

    def correlate(s, c):
        slot, size = s % 2, side * side * parts[c]
        x = split(out_ref[offsets[c] : offsets[c] + size, :])
        shape = (side, side, parts[c], half)
        cbuf[c][other] = three(dot, x, wide[slot, other], wide_low[slot, other]).reshape(shape)
        live[c] = remote(cbuf[c].at[other], cother[c], c_send.at[0, c], c_recv.at[0, c], partner)
        cbuf[c][core] = three(dot, x, wide[slot, core], wide_low[slot, core]).reshape(shape)

    def scatter_first(s, c):
        live[c].wait()
        cbuf[c][core] = cbuf[c][core] + cother[c][...]
        for d in range(1, side):
            src = cbuf[c].at[core, lax.rem(mx + d, side), :, :, pl.ds(0, quarter)]
            remote(src, rs1[c].at[d - 1], t_send.at[0, c], t_recv.at[0, c], at_x(d))
            src = cbuf[c].at[core, :, lax.rem(my + d, side), :, pl.ds(quarter, quarter)]
            remote(src, rs1[c].at[side - 2 + d], t_send.at[0, c], t_recv.at[0, c], at_y(d))
        live[c] = joint(rs1[c], t_send.at[0, c], t_recv.at[0, c])

    def scatter_second(s, c):
        live[c].wait()
        sum_x = cbuf[c][core, mx, :, :, :quarter]
        sum_y = cbuf[c][core, :, my, :, quarter:]
        for d in range(1, side):
            sum_x = sum_x + rs1[c][d - 1]
            sum_y = sum_y + rs1[c][side - 2 + d]
        t1x[c][...] = sum_x
        t1y[c][...] = sum_y
        for d in range(1, side):
            src = t1x[c].at[lax.rem(my + d, side)]
            remote(src, rs2[c].at[d - 1], t_send.at[1, c], t_recv.at[1, c], at_y(d))
            src = t1y[c].at[lax.rem(mx + d, side)]
            remote(src, rs2[c].at[side - 2 + d], t_send.at[1, c], t_recv.at[1, c], at_x(d))
        live[c] = joint(rs2[c], t_send.at[1, c], t_recv.at[1, c])

    def target(s, c):
        live[c].wait()
        sum_x = t1x[c][my]
        sum_y = t1y[c][mx]
        for d in range(1, side):
            sum_x = sum_x + rs2[c][d - 1]
            sum_y = sum_y + rs2[c][side - 2 + d]
        tfull[c][core, :, :quarter] = sum_x
        tfull[c][core, :, quarter:] = sum_y
        live[c] = remote(tfull[c].at[core], tfull[c].at[core], c_send.at[1, c], c_recv.at[1, c], partner)

    def solve(s, c):
        live[c].wait()
        slot = s % 2
        change = three(dot_back, split(tfull[c][0]), inv_high[slot, :, :half], inv_low[slot, :, :half])
        change += three(dot_back, split(tfull[c][1]), inv_high[slot, :, half:], inv_low[slot, :, half:])
        dfull[c][core, mx, my] = change * inv_rows
        for d in range(1, side):
            src = dfull[c].at[core, mx, my, :, pl.ds(0, quarter)]
            remote(src, src, t_send.at[2, c], t_recv.at[2, c], at_x(d))
            src = dfull[c].at[core, mx, my, :, pl.ds(quarter, quarter)]
            remote(src, src, t_send.at[2, c], t_recv.at[2, c], at_y(d))
        live[c] = joint(rs2[c], t_send.at[2, c], t_recv.at[2, c])

    def gather_second(s, c):
        live[c].wait()
        for d in range(1, side):
            src = dfull[c].at[core, :, my, :, pl.ds(0, quarter)]
            remote(src, src, t_send.at[3, c], t_recv.at[3, c], at_y(d))
            src = dfull[c].at[core, mx, :, :, pl.ds(quarter, quarter)]
            remote(src, src, t_send.at[3, c], t_recv.at[3, c], at_x(d))
        live[c] = joint(rs1[c], t_send.at[3, c], t_recv.at[3, c])

    def swap(s, c):
        live[c].wait()
        live[c] = remote(dfull[c].at[core], dfull[c].at[core], c_send.at[2, c], c_recv.at[2, c], partner)

    def update(s, c):
        live[c].wait()
        slot, size = s % 2, side * side * parts[c]
        gone = 0.0
        for h in range(2):
            d = split(dfull[c][h].reshape(size, half))
            gone = gone + three(dot_back, d, wide_back[slot, h], wide_low[slot, h])
        at = slice(offsets[c], offsets[c] + size)
        if s + 1 < STEPS:
            out_ref[at, :] = out_ref[at, :] - gone
            return
        last = out_ref[at, :] - gone
        r_back[:, at] = last[:, :rows].T
        w_back[:, :, at] = last[:, rows:].T.reshape(blocks, share, size)
        for k, (src, dst) in enumerate(((r_back.at[:, at], r_out.at[:, at]), (w_back.at[:, :, at], w_out.at[:, :, at]))):
            copy = pltpu.make_async_copy(src, dst, l_sem.at[3 + 2 * c + k])
            copy.start()
            stores.append(copy)

    phases = [correlate, scatter_first, scatter_second, target, solve, gather_second, swap, update]
    gathers = (inverse_first, inverse_second, inverse_third)
    for kind, s, c in schedule(parts, depth):
        if kind == PREPARE:
            prepare(s)
        elif kind >= GATHER:
            gathers[kind - GATHER](s)
        else:
            phases[kind](s, c)
    for copy in stores:
        copy.wait()


def body(side, depth, features, inverses, weights, residual, order, owner):
    rows, classes = residual.shape
    width = features.shape[2]
    half, quarter = width // 2, width // 4
    share = weights.shape[1]
    chips = side * side
    parts = plan(classes // chips)
    deep = rows + weights.shape[0] * share
    piece = rows // depth
    scratch = [
        pltpu.VMEM((share, width), F32),
        pltpu.VMEM(weights.shape, F32),
        pltpu.VMEM(residual.shape, F32),
        pltpu.VMEM(weights.shape, F32),
        pltpu.VMEM(residual.shape, F32),
        pltpu.VMEM((classes, deep), F32),
        pltpu.VMEM((depth, piece, width), F32),
        pltpu.VMEM((STEPS, piece, width), F32),
        pltpu.VMEM((STEPS, depth, piece, width), F32),
        pltpu.VMEM((depth, share, width), F32),
        pltpu.VMEM((STEPS, side, side, share, width), F32),
        pltpu.VMEM((2, 2, deep, half), BF16),
        pltpu.VMEM((2, 2, deep, half), BF16),
        pltpu.VMEM((2, 2, deep, half), BF16),
        pltpu.VMEM((2, half, width), BF16),
        pltpu.VMEM((2, half, width), BF16),
        pltpu.SemaphoreType.DMA((2 + STEPS,)),
        pltpu.SemaphoreType.DMA((2 + STEPS,)),
        pltpu.SemaphoreType.DMA((STEPS, 2)),
        pltpu.SemaphoreType.DMA((STEPS, 2)),
        pltpu.SemaphoreType.DMA((3, len(parts))),
        pltpu.SemaphoreType.DMA((3, len(parts))),
        pltpu.SemaphoreType.DMA((4, len(parts))),
        pltpu.SemaphoreType.DMA((4, len(parts))),
        pltpu.SemaphoreType.DMA((3 + 2 * len(parts),)),
    ]
    for shape in (
        lambda p: (2, side, side, p, half),
        lambda p: (side, side, p, half),
        lambda p: (2 * (side - 1), side, p, quarter),
        lambda p: (side, p, quarter),
        lambda p: (side, p, quarter),
        lambda p: (2 * (side - 1), p, quarter),
        lambda p: (2, p, half),
        lambda p: (2, side, side, p, half),
    ):
        scratch += [pltpu.VMEM(shape(p), F32) for p in parts]
    vmem = pl.BlockSpec(memory_space=pltpu.VMEM)
    smem = pl.BlockSpec(memory_space=pltpu.SMEM)
    hbm = pl.BlockSpec(memory_space=pl.ANY)
    return pl.pallas_call(
        functools.partial(kernel, side, depth, parts),
        out_shape=(jax.ShapeDtypeStruct(weights.shape, F32), jax.ShapeDtypeStruct(residual.shape, F32)),
        in_specs=[smem, smem, vmem, hbm, hbm, hbm],
        out_specs=(hbm, hbm),
        scratch_shapes=scratch,
        compiler_params=pltpu.CompilerParams(collective_id=0, has_side_effects=True, vmem_limit_bytes=60 << 20),
        cost_estimate=pl.CostEstimate(flops=14 * 10**9, bytes_accessed=8 * 10**6, transcendentals=0),
    )(order, owner, features, inverses, weights, residual)


def solution(mesh):
    side = {32: 4, 8: 2}[mesh.shape["rows"]]
    return jax.shard_map(
        functools.partial(body, side, mesh.shape["cls"]),
        mesh=mesh,
        in_specs=(
            P("cls", "rows", None),
            P("cls", None, None),
            P(None, "rows", "cls"),
            P("rows", "cls"),
            P(),
            P(),
        ),
        out_specs=(P(None, "rows", "cls"), P("rows", "cls")),
        check_vma=False,
    )
```

time: 200 us -> 163 us (0.81)
  Pallas kernels: 180 us -> 156 us
  local copies, waits for them, and re-layouts: 15 us -> 5.1 us
  other arithmetic: 3.81 us -> 0 us
    pallas_call x1, Pallas kernels: 180 us -> 156 us  [body(): pl.pallas_call(functools.partial(kernel, side, depth, parts), out_shape=(...]
    slice x3 -> x0, local copies, waits for them, and re-layouts: 6.01 us -> none  [body(): return (back[rows:].reshape(weights.shape), back[:rows])]
    transpose x1 -> x0, other arithmetic: 3.06 us -> none  [body(): state = jnp.concatenate([residual, stored], axis=0).T]
    reshape x1 -> x0, local copies, waits for them, and re-layouts: 2.24 us -> none  [body(): stored = weights.reshape(weights.shape[0] * share, classes)]
    unnamed x4 -> x2, local copies, waits for them, and re-layouts: 4.31 us -> 5.1 us
where the time goes in v2:
time: 163 us; the launch traced here: 162 us
  Pallas kernels  156 us (96%)
  local copies, waits for them, and re-layouts  5.1 us (3%)
    pallas_call x1, Pallas kernels, body(): pl.pallas_call(functools.partial(kernel, side, depth, parts), out_shape=(...  156 us
    unnamed x2, local copies, waits for them, and re-layouts  5.1 us

profile of v2, /device:TPU:1, one launch (start us, length us, event | category | flops | bytes accessed | tf_op | source)
XLA Modules:
  0.0 162.1 jit_solution(16014891633526548341)
XLA Ops:
  0.6 156.4 %shard_map.77 = (f32[8,16,1408]{2,1,0:T(8,128)}, f32[384,1408]{1,0:T(8,128)}) custom-call(s32[3]{0:T(128)} %chosen_ref.1, s32[8]{0:T(128)} %owner_ref.1, f32[1,384,512]{2,1,0:T(8,128)} %f_ref.1, f32[1,512,512]{2,1,0:T(8,128)} %all_inverse.1, f32[8,16,1408]{2,1,0:T(8,128)} %w_in.1, f32[384,1408]{1,0:T(8,128)} %r_in.1), custom_call_target="tpu_custom_call" | custom-call | flops 14000000000 | bytes 8000000 | tf_op jit(solution)/shard_map/pallas_call | solution.py:403
  157.0 2.0 %copy.10 = f32[8,16,1408]{2,1,0:T(8,128)} copy(f32[8,16,1408]{2,1,0:T(8,128)} %get-tuple-element.4) | data formatting | bytes 1441792
  159.0 3.1 %copy.11 = f32[384,1408]{1,0:T(8,128)} copy(f32[384,1408]{1,0:T(8,128)} %get-tuple-element.5) | data formatting | bytes 4325376

commit v3 on v2

--- a/solution.py
+++ b/solution.py
@@ -54,7 +54,10 @@
                 continue
             if phase == 4 and gather_place < 3 * s + 3:
                 continue
-            options.append((max(ready[c], now), place[c], phase, s, c))
+            start = max(ready[c], now)
+            if phase in (1, 5):
+                start = max(start, free[1])
+            options.append((start, -place[c], phase, s, c))
         if prepared < STEPS and (prepared < 2 or done[prepared - 2] == len(parts)):
             if any(p == prepared * PHASES for p in place):
                 options.append((max(block_ready[prepared], now), -1, PREPARE, prepared, 0))

time: 163 us -> 174 us (1.067)
  Pallas kernels: 156 us -> 168 us
    pallas_call x1, Pallas kernels: 156 us -> 168 us  [body(): pl.pallas_call(functools.partial(kernel, side, depth, parts), out_shape=(...]
where the time goes in v3:
time: 174 us; the launch traced here: 173 us
  Pallas kernels  168 us (97%)
  local copies, waits for them, and re-layouts  5.1 us (3%)
    pallas_call x1, Pallas kernels, body(): pl.pallas_call(functools.partial(kernel, side, depth, parts), out_shape=(...  168 us
    unnamed x2, local copies, waits for them, and re-layouts  5.1 us

profile of v3, /device:TPU:1, one launch (start us, length us, event | category | flops | bytes accessed | tf_op | source)
XLA Modules:
  0.0 173.5 jit_solution(8836229594345848231)
XLA Ops:
  0.6 167.8 %shard_map.77 = (f32[8,16,1408]{2,1,0:T(8,128)}, f32[384,1408]{1,0:T(8,128)}) custom-call(s32[3]{0:T(128)} %chosen_ref.1, s32[8]{0:T(128)} %owner_ref.1, f32[1,384,512]{2,1,0:T(8,128)} %f_ref.1, f32[1,512,512]{2,1,0:T(8,128)} %all_inverse.1, f32[8,16,1408]{2,1,0:T(8,128)} %w_in.1, f32[384,1408]{1,0:T(8,128)} %r_in.1), custom_call_target="tpu_custom_call" | custom-call | flops 14000000000 | bytes 8000000 | tf_op jit(solution)/shard_map/pallas_call | solution.py:406
  168.4 2.0 %copy.10 = f32[8,16,1408]{2,1,0:T(8,128)} copy(f32[8,16,1408]{2,1,0:T(8,128)} %get-tuple-element.4) | data formatting | bytes 1441792
  170.4 3.1 %copy.11 = f32[384,1408]{1,0:T(8,128)} copy(f32[384,1408]{1,0:T(8,128)} %get-tuple-element.5) | data formatting | bytes 4325376

commit v4 on v2

--- a/solution.py
+++ b/solution.py
@@ -26,7 +26,6 @@
 
 PHASES = 8
 PREPARE = 8
-GATHER = 9
 
 
 def schedule(parts, depth):
@@ -40,9 +39,8 @@
     now = 0.0
     ready = [0.0] * len(parts)
     place = [0] * len(parts)
-    gather_ready, gather_place = 6.0, 0
-    block_ready = [0.0] + [18.0 * s for s in range(1, STEPS)]
-    prepared, done, solved = 0, [0] * STEPS, [0] * STEPS
+    block_ready = [0.0] + [22.0 * s for s in range(1, STEPS)]
+    prepared, done = 0, [0] * STEPS
     order = []
     while min(place) < STEPS * PHASES:
         options = []
@@ -52,27 +50,15 @@
             s, phase = divmod(place[c], PHASES)
             if phase == 0 and prepared <= s:
                 continue
-            if phase == 4 and gather_place < 3 * s + 3:
-                continue
             options.append((max(ready[c], now), place[c], phase, s, c))
         if prepared < STEPS and (prepared < 2 or done[prepared - 2] == len(parts)):
-            if any(p == prepared * PHASES for p in place):
-                options.append((max(block_ready[prepared], now), -1, PREPARE, prepared, 0))
-        s, stage = divmod(gather_place, 3)
-        if s < STEPS and (stage < 2 or s < 2 or solved[s - 2] == len(parts)) and max(place) >= (s - 1) * PHASES + 2:
-            options.append((max(gather_ready, now), s * PHASES + 3, GATHER + stage, s, 0))
+            options.append((max(block_ready[prepared], now), -1, PREPARE, prepared, 0))
         start, _, kind, s, c = min(options)
         order.append((kind, s, c))
         now = start
         if kind == PREPARE:
             now += 1.0
             prepared += 1
-        elif kind >= GATHER:
-            now += 0.5
-            if kind < GATHER + 2:
-                free[1] = max(free[1], now) + (0.7, 2.6)[kind - GATHER]
-                gather_ready = free[1] + delay[1]
-            gather_place += 1
         else:
             now += compute[kind] * works[c] + fixed[kind]
             place[c] += 1
@@ -82,7 +68,6 @@
                 free[link] = max(free[link], now) + long * works[c]
                 ready[c] = free[link] + delay[link]
             done[s] += kind == PHASES - 1
-            solved[s] += kind == 4
     return order
 
 
@@ -209,10 +194,13 @@
 
     def inverse_third(s):
         joint(invf.at[s, pl.ds(0, side - 1)], i_send.at[s, 1], i_recv.at[s, 1]).wait()
-        slot = s % 2
         i_high, i_low = split(invf[s].reshape(half, 2 * half))
-        inv_high[slot] = i_high
-        inv_low[slot] = i_low
+        inv_high[s] = i_high
+        inv_low[s] = i_low
+
+    for gather in (inverse_first, inverse_second, inverse_third):
+        for s in range(STEPS):
+            gather(s)
 
     def dot(a, b):
         return jnp.dot(a, b, preferred_element_type=F32)
@@ -294,9 +282,8 @@
 
     def solve(s, c):
         live[c].wait()
-        slot = s % 2
-        change = three(dot_back, split(tfull[c][0]), inv_high[slot, :, :half], inv_low[slot, :, :half])
-        change += three(dot_back, split(tfull[c][1]), inv_high[slot, :, half:], inv_low[slot, :, half:])
+        change = three(dot_back, split(tfull[c][0]), inv_high[s, :, :half], inv_low[s, :, :half])
+        change += three(dot_back, split(tfull[c][1]), inv_high[s, :, half:], inv_low[s, :, half:])
         dfull[c][core, mx, my] = change * inv_rows
         for d in range(1, side):
             src = dfull[c].at[core, mx, my, :, pl.ds(0, quarter)]
@@ -338,12 +325,9 @@
             stores.append(copy)
 
     phases = [correlate, scatter_first, scatter_second, target, solve, gather_second, swap, update]
-    gathers = (inverse_first, inverse_second, inverse_third)
     for kind, s, c in schedule(parts, depth):
         if kind == PREPARE:
             prepare(s)
-        elif kind >= GATHER:
-            gathers[kind - GATHER](s)
         else:
             phases[kind](s, c)
     for copy in stores:
@@ -374,8 +358,8 @@
         pltpu.VMEM((2, 2, deep, half), BF16),
         pltpu.VMEM((2, 2, deep, half), BF16),
         pltpu.VMEM((2, 2, deep, half), BF16),
-        pltpu.VMEM((2, half, width), BF16),
-        pltpu.VMEM((2, half, width), BF16),
+        pltpu.VMEM((STEPS, half, width), BF16),
+        pltpu.VMEM((STEPS, half, width), BF16),
         pltpu.SemaphoreType.DMA((2 + STEPS,)),
         pltpu.SemaphoreType.DMA((2 + STEPS,)),
         pltpu.SemaphoreType.DMA((STEPS, 2)),

time: 163 us -> 171 us (1.049)
  Pallas kernels: 156 us -> 166 us
    pallas_call x1, Pallas kernels: 156 us -> 166 us  [body(): pl.pallas_call(functools.partial(kernel, side, depth, parts), out_shape=(...]
where the time goes in v4:
time: 171 us
  Pallas kernels  166 us (97%)
  local copies, waits for them, and re-layouts  5.1 us (3%)
    pallas_call x1, Pallas kernels, body(): pl.pallas_call(functools.partial(kernel, side, depth, parts), out_shape=(...  166 us
    unnamed x2, local copies, waits for them, and re-layouts  5.1 us

profile of v4, /device:TPU:1, one launch (start us, length us, event | category | flops | bytes accessed | tf_op | source)
XLA Modules:
  0.0 171.3 jit_solution(17094020252771815100)
XLA Ops:
  0.6 165.6 %shard_map.77 = (f32[8,16,1408]{2,1,0:T(8,128)}, f32[384,1408]{1,0:T(8,128)}) custom-call(s32[3]{0:T(128)} %chosen_ref.1, s32[8]{0:T(128)} %owner_ref.1, f32[1,384,512]{2,1,0:T(8,128)} %f_ref.1, f32[1,512,512]{2,1,0:T(8,128)} %all_inverse.1, f32[8,16,1408]{2,1,0:T(8,128)} %w_in.1, f32[384,1408]{1,0:T(8,128)} %r_in.1), custom_call_target="tpu_custom_call" | custom-call | flops 14000000000 | bytes 8000000 | tf_op jit(solution)/shard_map/pallas_call | solution.py:387
  166.2 2.0 %copy.10 = f32[8,16,1408]{2,1,0:T(8,128)} copy(f32[8,16,1408]{2,1,0:T(8,128)} %get-tuple-element.4) | data formatting | bytes 1441792
  168.2 3.1 %copy.11 = f32[384,1408]{1,0:T(8,128)} copy(f32[384,1408]{1,0:T(8,128)} %get-tuple-element.5) | data formatting | bytes 4325376
